TPU v7x, 512 devices: a whole 4x8x8 slice. The times are simulated.
512 devices in a mesh: span: 8 (over x, y_lo), seq: 64 (over y_hi, z, core).
Axes of the slice: x: 4, y: 8 (y_hi: 4, y_lo: 2; y = y_hi * 2 + y_lo), z: 8, core: 2. Of those that a mesh axis runs over, the one named last changes fastest.
Arguments:
- queries: bfloat16 [4096, 8192], P(('span', 'seq')), may hold values from -100 to 100
- keys: bfloat16 [4096, 8192], P(('span', 'seq')), may hold values from -6 to 6
- values: bfloat16 [4096, 8192], P(('span', 'seq')), may hold values from -24 to 24
- context: bfloat16 [2, 1024, 8192], P(None, 'span', 'seq'), may hold values from -12 to 12
- gate_table: float32 [64, 8192], P(None, 'seq'), may hold values from 0.1 to 1.9
- order: int32 [8], replicated, may hold values from 0 to 7, each once
- noise_step: int32 [8], replicated, may hold values from 0 to 63
- ctx_mask: int32 [8, 1024], replicated, may hold values from 0 to 1
Outputs:
- attended: bfloat16 [4096, 8192], P(('span', 'seq'))
All inputs are finite; a program needn't handle non-finite values.
Results may differ from a plain program's by a relative error of at most 0.004.
Values may be sent and summed in bfloat16 or wider, within the bound.
A program may use at most 64 MiB of HBM per device.

v0:
```python
import math

import jax
import jax.numpy as jnp
from jax import lax
from jax.sharding import PartitionSpec as P

NEG_FILL = -1e30


def attend_block(state_now, query_rows, key_block, value_block, visible, score_factor):
    row_peak, row_total, summed = state_now
    scores = (
        lax.dot_general(
            query_rows, key_block, (((1,), (1,)), ((), ())), preferred_element_type=jnp.float32
        )
        * score_factor
    )
    scores = jnp.where(visible[None, :], scores, NEG_FILL)
    new_peak = jnp.maximum(row_peak, jnp.max(scores, 1))
    rescale = jnp.exp(row_peak - new_peak)
    weights = jnp.where(visible[None, :], jnp.exp(scores - new_peak[:, None]), 0.0)
    row_total = row_total * rescale + jnp.sum(weights, 1)
    summed = summed * rescale[:, None] + jnp.dot(
        weights.astype(jnp.bfloat16), value_block, preferred_element_type=jnp.float32
    )
    return (new_peak, row_total, summed)


def attend_rows(state_now, query_rows, key_rows, value_rows, visible, score_factor):
    row_count = key_rows.shape[0]
    block_size = math.gcd(row_count, 1024)
    count_blocks = row_count // block_size

    def one_block(state_in, block_parts):
        key_block, value_block, block_seen = block_parts
        state_out = attend_block(
            state_in, query_rows, key_block, value_block, block_seen, score_factor
        )
        return (state_out, None)

    shaped = (
        key_rows.reshape(count_blocks, block_size, key_rows.shape[1]),
        value_rows.reshape(count_blocks, block_size, value_rows.shape[1]),
        visible.reshape(count_blocks, block_size),
    )
    state_out, unused = lax.scan(one_block, state_now, shaped)
    return state_out


def local(queries, keys, values, context, gate_table, order, noise_step, ctx_mask):
    seq_count = lax.axis_size("seq")
    span_count = lax.axis_size("span")
    own_span = lax.axis_index("span")
    tok_rows, full_width = queries.shape
    head_width = full_width // seq_count
    span_rows = tok_rows * seq_count
    score_factor = head_width ** (-0.5)
    span_ids = jnp.arange(span_count, dtype=jnp.int32)
    is_own = span_ids == own_span
    own_order = jnp.sum(jnp.where(is_own, order, 0))
    span_seen = (order < own_order) | is_own
    ctx_seen = jnp.sum(jnp.where(is_own[:, None], ctx_mask, 0), 0) == 1
    start_state = (
        jnp.full((span_rows,), NEG_FILL, jnp.float32),
        jnp.zeros((span_rows,), jnp.float32),
        jnp.zeros((span_rows, head_width), jnp.float32),
    )
    query_heads, key_heads, value_heads = (
        lax.all_to_all(queries, "seq", split_axis=1, concat_axis=0, tiled=True),
        lax.all_to_all(keys, "seq", split_axis=1, concat_axis=0, tiled=True),
        lax.all_to_all(values, "seq", split_axis=1, concat_axis=0, tiled=True),
    )
    key_rows = lax.all_gather(context[0], "span", axis=0, tiled=True)
    value_rows = lax.all_gather(context[1], "span", axis=0, tiled=True)
    state_now = attend_rows(start_state, query_heads, key_rows, value_rows, ctx_seen, score_factor)
    key_rows = lax.all_gather(key_heads, "span", axis=0, tiled=True)
    value_rows = lax.all_gather(value_heads, "span", axis=0, tiled=True)
    row_ids = jnp.arange(key_rows.shape[0], dtype=jnp.int32) // span_rows
    state_now = attend_rows(
        state_now,
        query_heads,
        key_rows,
        value_rows,
        jnp.any((row_ids[:, None] == span_ids[None, :]) & span_seen[None, :], 1),
        score_factor,
    )
    row_peak, row_total, summed = state_now
    step_now = jnp.sum(jnp.where(is_own, noise_step, 0))
    steps_count = gate_table.shape[0]
    step_ids = jnp.arange(steps_count, dtype=jnp.int32)
    gate_row = jnp.sum(jnp.where((step_ids == step_now)[:, None], gate_table, 0.0), 0)
    mixture = summed / row_total[:, None]
    gated = (mixture * gate_row[None, :]).astype(jnp.bfloat16)
    return lax.all_to_all(gated, "seq", split_axis=0, concat_axis=1, tiled=True)


def solution(mesh):
    placed = (
        P(("span", "seq"), None),
        P(("span", "seq"), None),
        P(("span", "seq"), None),
        P(None, "span", "seq"),
        P(None, "seq"),
        P(),
        P(),
        P(),
    )
    return jax.shard_map(
        local, mesh=mesh, in_specs=placed, out_specs=P(("span", "seq"), None), check_vma=False
    )
```

profile of v0, /device:TPU:1, one launch (start us, length us, event | category | flops | bytes accessed | tf_op | source)
XLA Modules:
  0.0 215.1 jit_solution(6657385108374621851)
XLA Ops:
  6.5 30.3 %all_to_all.76 = bf16[8,64,128]{2,0,1:T(8,128)(2,1)} all-to-all(bf16[8,64,128]{2,0,1:T(8,128)(2,1)} %bitcast.51), channel_id=1, replica_groups=mesh['span'=8,'seq'=64] {'seq'}, dimensions={1} | all-to-all | bytes 262144 | tf_op jit(solution)/shard_map/all_to_all | solution.py:71
  36.9 4.6 %all-to-all-start.2 = ((bf16[8,64,128]{2,0,1:T(8,128)(2,1)}), bf16[8,64,128]{2,0,1:T(8,128)(2,1)S(1)}, u32[]{:S(2)}, u32[]{:S(2)}) async-start(bf16[8,64,128]{2,0,1:T(8,128)(2,1)} %bitcast.52), calls=%async_computation.2 | async-start | bytes 262144 | tf_op jit(solution)/shard_map/all_to_all | solution.py:72
  41.5 1.3 select_reduce_fusion.3
  42.8 1.3 compare_or_fusion
  44.1 0.8 select_reduce_fusion.1
  44.9 0.8 fusion.40
  45.7 1.4 select_reduce_fusion.2
  47.1 25.9 %all-gather = bf16[1,1024,128]{2,1,0:T(8,128)(2,1)S(1)} all-gather(bf16[1,128,128]{2,1,0:T(8,128)(2,1)S(1)} %get-tuple-element.95), channel_id=2, replica_groups=mesh['span'=8,'seq'=64] {'span'}, dimensions={1}, use_global_device_ids=true | all-gather | bytes 294912 | tf_op jit(solution)/shard_map/all_gather | solution.py:74
  73.0 22.6 %all-gather.1 = bf16[1,1024,128]{2,1,0:T(8,128)(2,1)S(1)} all-gather(bf16[1,128,128]{2,1,0:T(8,128)(2,1)S(1)} %get-tuple-element.94), channel_id=3, replica_groups=mesh['span'=8,'seq'=64] {'span'}, dimensions={1}, use_global_device_ids=true | all-gather | bytes 294912 | tf_op jit(solution)/shard_map/all_gather | solution.py:75
  95.6 22.8 %all-to-all-start = ((bf16[8,64,128]{2,0,1:T(8,128)(2,1)}), bf16[8,64,128]{2,0,1:T(8,128)(2,1)S(1)}, u32[]{:S(2)}, u32[]{:S(2)}) async-start(bf16[8,64,128]{2,0,1:T(8,128)(2,1)} %bitcast.53), calls=%async_computation | async-start | bytes 262144 | tf_op jit(solution)/shard_map/all_to_all | solution.py:70
  118.5 0.7 all-gather.7.cloned.1.call-update
  119.2 0.7 iota_compare_fusion.1
  120.0 0.8 select_reduce_fusion
  120.8 10.1 %all-to-all-done = bf16[8,64,128]{2,0,1:T(8,128)(2,1)S(1)} async-done(((bf16[8,64,128]{2,0,1:T(8,128)(2,1)}), bf16[8,64,128]{2,0,1:T(8,128)(2,1)S(1)}, u32[]{:S(2)}, u32[]{:S(2)}) %all-to-all-start) | async-done | bytes 131104 | tf_op jit(solution)/shard_map/all_to_all | solution.py:70
  131.5 0.6 fusion.20
  132.1 0.6 convolution_add_fusion.1
  132.8 28.8 %all-gather.7.cloned.1.call-done = bf16[4096,128]{1,0:T(8,128)(2,1)} async-done(((bf16[512,128]{1,0:T(8,128)(2,1)}), bf16[4096,128]{1,0:T(8,128)(2,1)}) %all-gather.7.cloned.1.call-update) | async-done | bytes 1048592 | tf_op jit(solution)/shard_map/all_gather | solution.py:78
  161.6 16.0 %while.2 = (s32[]{:T(128)}, f32[512]{0:T(512)S(1)}, f32[512]{0:T(512)S(1)}, f32[512,128]{1,0:T(8,128)S(1)}, pred[4,1024]{1,0:T(4,128)(4,1)S(1)}, /*index=5*/bf16...) while((s32[]{:T(128)}, f32[512]{0:T(512)S(1)}, ...), condition=%wide.region_8.9_spmd, body=%wide.region_5.8_spmd.sunk | while | flops 275383296 | bytes 7510113 | solution.py:47
  161.6 1.4 fusion.50
  163.0 0.6 fusion.51
  163.6 1.9 convolution_add_fusion.3
  165.6 1.4 fusion.50
  167.0 0.6 fusion.51
  167.6 1.9 convolution_add_fusion.3
  169.6 1.4 fusion.50
  171.0 0.6 fusion.51
  171.6 1.9 convolution_add_fusion.3
  173.6 1.4 fusion.50
  175.0 0.6 fusion.51
  175.6 1.9 convolution_add_fusion.3
  177.7 29.9 %all_to_all.77 = bf16[64,8,128]{2,1,0:T(8,128)(2,1)S(1)} all-to-all(bf16[64,8,128]{2,1,0:T(8,128)(2,1)S(1)} %fusion.29), channel_id=1, replica_groups=mesh['span'=8,'seq'=64] {'seq'}, dimensions={0} | all-to-all | bytes 262144 | tf_op jit(solution)/shard_map/all_to_all | solution.py:95
  207.6 0.7 copy.24
  (31 shorter events, 1.1 us)
Async XLA Ops:
  6.5 126.2 %all-gather.5.cloned.1.call-start = ((), (), s32[]{:S(2)}) async-start(), calls=%async_computation.4 | async-start | bytes 1179648 | tf_op jit(solution)/shard_map/all_gather | solution.py:77
  36.9 58.7 %all-to-all-start.2 = ((bf16[8,64,128]{2,0,1:T(8,128)(2,1)}), bf16[8,64,128]{2,0,1:T(8,128)(2,1)S(1)}, u32[]{:S(2)}, u32[]{:S(2)}) async-start(bf16[8,64,128]{2,0,1:T(8,128)(2,1)} %bitcast.52), calls=%async_computation.2 | async-start | bytes 262144 | tf_op jit(solution)/shard_map/all_to_all | solution.py:72
  95.6 22.9 %copy-start = (bf16[8,64,128]{2,0,1:T(8,128)(2,1)}, bf16[8,64,128]{2,0,1:T(8,128)(2,1)S(1)}, u32[]{:S(2)}) copy-start(bf16[8,64,128]{2,0,1:T(8,128)(2,1)S(1)} %all-to-all-done.2) | copy-start | bytes 393220
  95.6 35.4 %all-to-all-start = ((bf16[8,64,128]{2,0,1:T(8,128)(2,1)}), bf16[8,64,128]{2,0,1:T(8,128)(2,1)S(1)}, u32[]{:S(2)}, u32[]{:S(2)}) async-start(bf16[8,64,128]{2,0,1:T(8,128)(2,1)} %bitcast.53), calls=%async_computation | async-start | bytes 262144 | tf_op jit(solution)/shard_map/all_to_all | solution.py:70
  118.4 43.2 %all-gather.7.cloned.1.call-start = ((), (), s32[]{:S(2)}) async-start(), calls=%async_computation.5 | async-start | bytes 1179648 | tf_op jit(solution)/shard_map/all_gather | solution.py:78
Sparse Core Ops, SparseCore 0:
  37.0 36.8 all-gather.4
  121.3 40.2 all-gather.6
where the time goes:
time: 216 us; the launch traced here: 215 us
  blocking collectives  109 us (50%)
  waiting for transfers between devices  39.7 us (18%)
  starting transfers between devices  27.4 us (13%)
  matrix products  14.4 us (7%)
  between operations  13.5 us (6%)
  other arithmetic  9.62 us (4%)
    all_to_all x1, blocking collectives, local(): lax.all_to_all(keys, 'seq', split_axis=1, concat_axis=0, tiled=True)  30.3 us
    all_to_all x1, blocking collectives, local(): return lax.all_to_all(gated, 'seq', split_axis=0, concat_axis=1, tiled=True)  29.9 us
    all_gather x1, waiting for transfers between devices, local(): value_rows = lax.all_gather(value_heads, 'span', axis=0, tiled=True)  28.8 us
    all_gather x1, blocking collectives, local(): key_rows = lax.all_gather(context[0], 'span', axis=0, tiled=True)  25.9 us
    all_to_all x1, starting transfers between devices, local(): lax.all_to_all(queries, 'seq', split_axis=1, concat_axis=0, tiled=True)  22.8 us
    all_gather x1, blocking collectives, local(): value_rows = lax.all_gather(context[1], 'span', axis=0, tiled=True)  22.6 us
    all_to_all x1, waiting for transfers between devices, local(): lax.all_to_all(queries, 'seq', split_axis=1, concat_axis=0, tiled=True)  10.1 us
    dot_general x5, matrix products, attend_block(): jnp.dot(weights.astype(jnp.bfloat16), value_block, preferred_element_type...  8.28 us
  transfers between devices with their start and end apart: 4, of which 2 were waited for; matrix products, arithmetic and copies ran while one was open for 4% of the time, Pallas kernels for 0%

commit v1 on v0

v1 whole, which is shorter than its diff:
```python
import jax
import jax.numpy as jnp
from jax import lax
from jax.experimental import pallas as pl
from jax.experimental.pallas import tpu as pltpu
from jax.sharding import PartitionSpec as P

MESH = pl.DeviceIdType.MESH
NEG_FILL = -1e30
LOG2E = 1.4426950408889634
HD = 128
GROUP_ORDER = (1, 4, 2, 3)


def kernel(q_hbm, k_hbm, v_hbm, ctx_hbm, gate_hbm, order_hbm, step_hbm, mask_hbm, out_ref,
           q_in, k_in, v_in, ctx_in, gate_in, order_s, step_s, mask_in,
           kv_out, ctx_out, kv, q_rows, gate_sib, out_rows, ctx_bias,
           load_sem, own_sem, left_sem, right_sem, far_sem, sib_sem, misc_sem, send_sem):
    span, seq = lax.axis_index("span"), lax.axis_index("seq")
    x, yl = span // 2, span % 2
    yh, z, k = seq // 16, (seq // 2) % 8, seq % 2
    y = yh * 2 + yl
    stays = yl == k
    own = x * 2 + k
    left_x, right_x, far_x = (x + 3) % 4, (x + 1) % 4, (x + 2) % 4

    def device(x_, y_, z_, k_):
        return (x_ * 2 + y_ % 2, (y_ // 2) * 16 + z_ * 2 + k_)

    left, right = device(left_x, y, z, k), device(right_x, y, z, k)
    sibling = device(x, y, z, 1 - k)

    def remote(src, dst, sent, got, to):
        return pltpu.make_async_remote_copy(
            src_ref=src, dst_ref=dst, send_sem=sent, recv_sem=got, device_id=to, device_id_type=MESH
        )

    def wait_for(ref, sem):
        pltpu.make_async_copy(ref, ref, sem).wait()

    def far_first(i):
        return 4 + (1 - 2 * (i % 2)) * ((i + 1) // 2)

    loads = [
        pltpu.make_async_copy(src, dst, load_sem.at[i])
        for i, (src, dst) in enumerate(
            [(k_hbm, k_in), (v_hbm, v_in), (ctx_hbm, ctx_in), (q_hbm, q_in), (gate_hbm, gate_in),
             (order_hbm, order_s), (step_hbm, step_s), (mask_hbm, mask_in)]
        )
    ]
    for load in loads:
        load.start()

    barrier = pltpu.get_barrier_semaphore()

    def greet(j, carry):
        z_, y_, k_ = (z + far_first(j // 8)) % 8, (yh + 2 + (j // 2) % 4) % 4 * 2 + k, j % 2

        @pl.when((z_ != z) | (y_ != y) | (k_ != k))
        def _():
            pl.semaphore_signal(barrier, inc=1, device_id=device(x, y_, z_, k_), device_id_type=MESH)

        return carry

    lax.fori_loop(0, 64, greet, 0)
    for to in (left, right, sibling):
        pl.semaphore_signal(barrier, inc=1, device_id=to, device_id_type=MESH)

    for load in loads[:3]:
        load.wait()
    for h in range(64):
        kv_out[h, 0] = k_in[:, h * HD:(h + 1) * HD]
        kv_out[h, 1] = v_in[:, h * HD:(h + 1) * HD]
    ctx_out[...] = ctx_in[...].reshape(ctx_out.shape)
    for load in loads[3:]:
        load.wait()

    @pl.when(stays)
    def _():
        pl.semaphore_wait(barrier, 66)

    @pl.when(jnp.logical_not(stays))
    def _():
        pl.semaphore_wait(barrier, 67)

    gate_copy = remote(gate_in, gate_sib, misc_sem.at[0], misc_sem.at[1], sibling)
    gate_copy.start()

    @pl.when(stays)
    def _():
        pltpu.make_async_copy(ctx_out, kv.at[:, own, 0], own_sem.at[0]).start()

    @pl.when(jnp.logical_not(stays))
    def _():
        remote(ctx_out, kv.at[:, span, 0], send_sem.at[0], own_sem.at[0], device(x, yh * 2 + k, z, yl)).start()

    def send_group(g):
        def send_one(j, carry):
            z_, y_ = (z + far_first(j // 2)) % 8, (y + 8 - 2 * g - j % 2) % 8
            h = (y_ // 2) * 16 + z_ * 2 + y_ % 2
            dst = kv.at[:, span, 1 + g, z * 2 + k]
            here = stays & (y_ == y) & (z_ == z)

            @pl.when(here)
            def _():
                pltpu.make_async_copy(kv_out.at[h], dst, own_sem.at[1 + g]).start()

            @pl.when(jnp.logical_not(here))
            def _():
                remote(kv_out.at[h], dst, send_sem.at[1], own_sem.at[1 + g], device(x, y_, z_, yl)).start()

            return carry

        lax.fori_loop(0, 16, send_one, 0)

    for slot in GROUP_ORDER:
        send_group(slot - 1)

    def to_sibling(ref, kind):
        remote(ref, ref, send_sem.at[4], sib_sem.at[kind], sibling).start()

    def pass_own(slot):
        ref = kv.at[:, own, slot]
        wait_for(ref, own_sem.at[slot])
        remote(ref, ref, send_sem.at[3], left_sem.at[slot], right).start()
        remote(ref, ref, send_sem.at[3], right_sem.at[slot], left).start()
        to_sibling(ref, 0)

    def pass_near(slot):
        from_left, from_right = kv.at[:, left_x * 2 + k, slot], kv.at[:, right_x * 2 + k, slot]
        wait_for(from_left, left_sem.at[slot])
        half = kv.at[0, left_x * 2 + k, slot]
        remote(half, half, send_sem.at[3], far_sem.at[slot, 0], right).start()
        to_sibling(from_left, 1)
        wait_for(from_right, right_sem.at[slot])
        half = kv.at[1, right_x * 2 + k, slot]
        remote(half, half, send_sem.at[3], far_sem.at[slot, 1], left).start()
        to_sibling(from_right, 2)

    def pass_far(slot):
        ref = kv.at[:, far_x * 2 + k, slot]
        wait_for(kv.at[0, far_x * 2 + k, slot], far_sem.at[slot, 0])
        wait_for(kv.at[1, far_x * 2 + k, slot], far_sem.at[slot, 1])
        to_sibling(ref, 3)

    pass_own(0)

    def send_query(j, carry):
        z_, y_ = (z + far_first(j // 8)) % 8, (y + 4 + j) % 8
        h = (y_ // 2) * 16 + z_ * 2 + y_ % 2
        src = q_in.at[:, pl.ds(pl.multiple_of(h * HD, HD), HD)]
        dst = q_rows.at[seq]
        here = stays & (y_ == y) & (z_ == z)

        @pl.when(here)
        def _():
            pltpu.make_async_copy(src, dst, misc_sem.at[2]).start()

        @pl.when(jnp.logical_not(here))
        def _():
            remote(src, dst, send_sem.at[2], misc_sem.at[2], device(x, y_, z_, yl)).start()

        return carry

    lax.fori_loop(0, 64, send_query, 0)

    pass_own(1)
    pass_near(0)
    pass_own(4)
    pass_near(1)
    pass_own(2)
    pass_near(4)
    pass_own(3)

    scale = (HD ** -0.5) * LOG2E
    own_order = order_s[own]
    is_own = lax.broadcasted_iota(jnp.int32, (8, HD), 0) == own
    for s in range(8):
        seen = jnp.sum(jnp.where(is_own, mask_in[:, s * HD:(s + 1) * HD], 0), 0, keepdims=True)
        ctx_bias[s:s + 1, :] = jnp.where(seen == 1, 0.0, NEG_FILL)

    def bias_of(x_):
        parts = []
        for c in range(2):
            s = x_ * 2 + c
            parts.append(ctx_bias[pl.ds(s, 1), :])
            visible = (order_s[s] < own_order) | (s == own)
            parts.append(jnp.full((1, 512), jnp.where(visible, 0.0, NEG_FILL), jnp.float32))
        return jnp.concatenate(parts, axis=1)

    def attend(state, x_):
        keys = kv[0, pl.ds(x_ * 2, 2)].reshape(1280, HD)
        values = kv[1, pl.ds(x_ * 2, 2)].reshape(1280, HD)
        scores = lax.dot_general(queries, keys, (((1,), (1,)), ((), ())), preferred_element_type=jnp.float32)
        scores = scores * scale + bias_of(x_)
        peak = jnp.max(scores, 1, keepdims=True)
        if state is not None:
            peak = jnp.maximum(state[0], peak)
        weights = jnp.exp2(scores - peak)
        total = weights[:, 0:HD]
        for t in range(1, 10):
            total = total + weights[:, t * HD:(t + 1) * HD]
        mixed = jnp.dot(weights.astype(jnp.bfloat16), values, preferred_element_type=jnp.float32)
        if state is not None:
            rescale = jnp.exp2(state[0] - peak)
            total = total + state[1] * rescale
            mixed = mixed + state[2] * rescale
        return peak, total, mixed

    def sibling_has_sent(kind):
        wait_for(kv.at[:, 0], sib_sem.at[kind])

    wait_for(q_rows, misc_sem.at[2])
    queries = q_rows[...].reshape(512, HD)
    sibling_has_sent(0)
    state = attend(None, x)
    pass_near(2)
    pass_near(3)
    sibling_has_sent(1)
    state = attend(state, left_x)
    for slot in (0, 1, 4, 2):
        pass_far(slot)
    sibling_has_sent(2)
    state = attend(state, right_x)
    pass_far(3)
    sibling_has_sent(3)
    _, total, mixed = attend(state, far_x)

    gate_copy.wait()
    step = step_s[own]
    gate = jnp.where(stays, gate_in[pl.ds(step, 1), :], gate_sib[pl.ds(step, 1), :])
    mixture = mixed / jnp.sum(total, 1, keepdims=True)
    out_rows[...] = (mixture * gate).astype(jnp.bfloat16).reshape(out_rows.shape)

    head = yh * 16 + z * 2 + yl
    dst = out_ref.at[:, pl.ds(pl.multiple_of(head * HD, HD), HD)]

    def send_back(j, carry):
        z_, yh_, k_ = (z + far_first(j // 8)) % 8, (yh + 2 + (j // 2) % 4) % 4, j % 2
        src = out_rows.at[yh_ * 16 + z_ * 2 + k_]
        here = stays & (yh_ == yh) & (z_ == z) & (k_ == k)

        @pl.when(here)
        def _():
            pltpu.make_async_copy(src, dst, misc_sem.at[3]).start()

        @pl.when(jnp.logical_not(here))
        def _():
            remote(src, dst, send_sem.at[5], misc_sem.at[3], device(x, yh_ * 2 + k, z_, k_)).start()

        return carry

    lax.fori_loop(0, 64, send_back, 0)

    wait_for(kv.at[:, pl.ds(0, 3)], send_sem.at[3])
    wait_for(kv.at[:, pl.ds(0, 4)], send_sem.at[4])

    @pl.when(stays)
    def _():
        wait_for(kv_out.at[pl.ds(0, 63)], send_sem.at[1])
        wait_for(q_rows.at[pl.ds(0, 63)], send_sem.at[2])
        wait_for(out_rows.at[pl.ds(0, 63)], send_sem.at[5])

    @pl.when(jnp.logical_not(stays))
    def _():
        wait_for(ctx_out, send_sem.at[0])
        wait_for(kv_out, send_sem.at[1])
        wait_for(q_rows, send_sem.at[2])
        wait_for(out_rows, send_sem.at[5])

    wait_for(out_rows, misc_sem.at[3])


def local(*args):
    bf16 = jnp.bfloat16
    any_space = pl.BlockSpec(memory_space=pl.ANY)
    dma = pltpu.SemaphoreType.DMA
    return pl.pallas_call(
        kernel,
        out_shape=jax.ShapeDtypeStruct((8, 8192), bf16),
        in_specs=[any_space] * 8,
        out_specs=pl.BlockSpec(memory_space=pltpu.VMEM),
        scratch_shapes=[
            pltpu.VMEM((8, 8192), bf16),
            pltpu.VMEM((8, 8192), bf16),
            pltpu.VMEM((8, 8192), bf16),
            pltpu.VMEM((2, 128, HD), bf16),
            pltpu.VMEM((64, HD), jnp.float32),
            pltpu.SMEM((8,), jnp.int32),
            pltpu.SMEM((8,), jnp.int32),
            pltpu.VMEM((8, 1024), jnp.int32),
            pltpu.VMEM((64, 2, 8, HD), bf16),
            pltpu.VMEM((2, 16, 8, HD), bf16),
            pltpu.VMEM((2, 8, 5, 16, 8, HD), bf16),
            pltpu.VMEM((64, 8, HD), bf16),
            pltpu.VMEM((64, HD), jnp.float32),
            pltpu.VMEM((64, 8, HD), bf16),
            pltpu.VMEM((8, 128), jnp.float32),
            dma((8,)),
            dma((5,)),
            dma((5,)),
            dma((5,)),
            dma((5, 2)),
            dma((4,)),
            dma((4,)),
            dma((6,)),
        ],
        compiler_params=pltpu.CompilerParams(
            collective_id=0, has_side_effects=True, vmem_limit_bytes=48 << 20
        ),
        cost_estimate=pl.CostEstimate(flops=1342177280, bytes_accessed=1 << 20, transcendentals=2621440),
        name="span_attention",
    )(*args)


def solution(mesh):
    rows = P(("span", "seq"), None)
    placed = (rows, rows, rows, P(None, "span", "seq"), P(None, "seq"), P(), P(), P())
    return jax.shard_map(local, mesh=mesh, in_specs=placed, out_specs=rows, check_vma=False)
```

time: 216 us -> 59 us (0.27)
  blocking collectives: 109 us -> 0 us
  Pallas kernels: 0 us -> 51.5 us
  waiting for transfers between devices: 39.7 us -> 0 us
  starting transfers between devices: 27.4 us -> 0 us
  matrix products: 14.4 us -> 0 us
  between operations: 13.5 us -> 0.02 us
  other arithmetic: 9.62 us -> 0 us
  local copies, waits for them, and re-layouts: 1.58 us -> 7.03 us
    all_to_all x2 -> x0, blocking collectives: 60.2 us -> none  [the longest x1 30.3 us: local(): lax.all_to_all(keys, 'seq', split_axis=1, concat_axis=0, tiled=True)]
    pallas_call x0 -> x1, Pallas kernels: none -> 51.5 us  [local(): pl.pallas_call(kernel, out_shape=jax.ShapeDtypeStruct((8, 8192), bf16), i...]
    all_gather x2 -> x0, blocking collectives: 48.5 us -> none  [the longest x1 25.9 us: local(): key_rows = lax.all_gather(context[0], 'span', axis=0, tiled=True)]
    all_gather x2 -> x0, waiting for transfers between devices: 28.9 us -> none  [the longest x1 28.8 us: local(): value_rows = lax.all_gather(value_heads, 'span', axis=0, tiled=True)]
    all_to_all x2 -> x0, starting transfers between devices: 27.4 us -> none  [the longest x1 22.8 us: local(): lax.all_to_all(queries, 'seq', split_axis=1, concat_axis=0, tiled=True)]
    dot_general x10 -> x0, matrix products: 14.4 us -> none  [the longest x5 8.28 us: attend_block(): jnp.dot(weights.astype(jnp.bfloat16), value_block, preferred_element_type...]
    all_to_all x2 -> x0, waiting for transfers between devices: 10.1 us -> none  [the longest x1 10.1 us: local(): lax.all_to_all(queries, 'seq', split_axis=1, concat_axis=0, tiled=True)]
    reduce_sum x9 -> x0, other arithmetic: 7.27 us -> none  [the longest x5 2.93 us: attend_block(): row_total = row_total * rescale + jnp.sum(weights, 1)]
  transfers between devices with their start and end apart: 4 -> 0, of which waited for: 2 -> 0; matrix products, arithmetic and copies ran while one was open for 4% -> 0% of each run, Pallas kernels for 0% -> 0%
where the time goes in v1:
time: 59 us; the launch traced here: 58.6 us
  Pallas kernels  51.5 us (87%)
  local copies, waits for them, and re-layouts  7.03 us (12%)
    pallas_call x1, Pallas kernels, local(): pl.pallas_call(kernel, out_shape=jax.ShapeDtypeStruct((8, 8192), bf16), i...  51.5 us
    unnamed x17, local copies, waits for them, and re-layouts  7.03 us

profile of v1, /device:TPU:1, one launch (start us, length us, event | category | flops | bytes accessed | tf_op | source)
XLA Modules:
  0.0 58.6 jit_solution(12685390814970311657)
XLA Ops:
  0.0 0.0 copy-start
  0.0 0.9 %copy-done = bf16[8,8192]{1,0:T(8,128)(2,1)S(1)} copy-done((bf16[8,8192]{1,0:T(8,128)(2,1)S(1)}, bf16[8,8192]{1,0:T(8,128)(2,1)}, u32[]{:S(2)}) %copy-start) | copy-done | bytes 131096
  0.9 0.0 copy-start.1
  0.9 0.9 %copy-done.1 = bf16[8,8192]{1,0:T(8,128)(2,1)S(1)} copy-done((bf16[8,8192]{1,0:T(8,128)(2,1)S(1)}, bf16[8,8192]{1,0:T(8,128)(2,1)}, u32[]{:S(2)}) %copy-start.1) | copy-done | bytes 131096
  1.8 0.0 copy-start.2
  1.8 0.9 %copy-done.2 = bf16[8,8192]{1,0:T(8,128)(2,1)S(1)} copy-done((bf16[8,8192]{1,0:T(8,128)(2,1)S(1)}, bf16[8,8192]{1,0:T(8,128)(2,1)}, u32[]{:S(2)}) %copy-start.2) | copy-done | bytes 131096
  2.7 0.0 copy-start.3
  2.7 0.8 %copy-done.3 = bf16[2,128,128]{2,1,0:T(8,128)(2,1)S(1)} copy-done((bf16[2,128,128]{2,1,0:T(8,128)(2,1)S(1)}, bf16[2,128,128]{2,1,0:T(8,128)(2,1)}, u32[]{:S(2)}) %copy-start.3) | copy-done | bytes 65560
  3.6 0.0 copy-start.4
  3.6 0.8 %copy-done.4 = f32[64,128]{1,0:T(8,128)S(1)} copy-done((f32[64,128]{1,0:T(8,128)S(1)}, f32[64,128]{1,0:T(8,128)}, u32[]{:S(2)}) %copy-start.4) | copy-done | bytes 32792
  4.3 0.0 copy-start.5
  4.3 0.8 %copy-done.5 = s32[8,1024]{1,0:T(8,128)S(1)} copy-done((s32[8,1024]{1,0:T(8,128)S(1)}, s32[8,1024]{1,0:T(8,128)}, u32[]{:S(2)}) %copy-start.5) | copy-done | bytes 32792
  5.1 0.0 copy-start.6
  5.1 0.7 %copy-done.6 = s32[8]{0:T(128)S(1)} copy-done((s32[8]{0:T(128)S(1)}, s32[8]{0:T(128)}, u32[]{:S(2)}) %copy-start.6) | copy-done | bytes 56
  5.7 0.0 copy-start.7
  5.7 0.7 %copy-done.7 = s32[8]{0:T(128)S(1)} copy-done((s32[8]{0:T(128)S(1)}, s32[8]{0:T(128)}, u32[]{:S(2)}) %copy-start.7) | copy-done | bytes 56
  6.4 51.5 %span_attention.1 = bf16[8,8192]{1,0:T(8,128)(2,1)S(1)} custom-call(bf16[8,8192]{1,0:T(8,128)(2,1)S(1)} %copy-done, bf16[8,8192]{1,0:T(8,128)(2,1)S(1)} %copy-done.1, bf16[8,8192]{1,0:T(8,128)(2,1)S(1)} %copy-done.2, bf16[2,128,128]{2,1,0:T(8,128)(2,1)S(1)} %copy-done.3, f32[64,128]{1,0:T(8,128)S(1)} %copy-done.4, s32[8]{0:T(128)S(1)} %copy-done.6, ...), custom_call_target="tpu_custom_call" | custom-call | flops 1342177280 | bytes 1048576 | tf_op jit(solution)/shard_map/span_attention/pallas_call | solution.py:278
  57.9 0.7 %copy.10 = bf16[8,8192]{1,0:T(8,128)(2,1)} copy(bf16[8,8192]{1,0:T(8,128)(2,1)S(1)} %span_attention.1) | data formatting | bytes 262144
Async XLA Ops:
  0.0 0.9 %copy-start = (bf16[8,8192]{1,0:T(8,128)(2,1)S(1)}, bf16[8,8192]{1,0:T(8,128)(2,1)}, u32[]{:S(2)}) copy-start(bf16[8,8192]{1,0:T(8,128)(2,1)} %q_hbm.1) | copy-start | bytes 393220
  0.9 0.9 %copy-start.1 = (bf16[8,8192]{1,0:T(8,128)(2,1)S(1)}, bf16[8,8192]{1,0:T(8,128)(2,1)}, u32[]{:S(2)}) copy-start(bf16[8,8192]{1,0:T(8,128)(2,1)} %k_hbm.1) | copy-start | bytes 393220
  1.8 0.9 %copy-start.2 = (bf16[8,8192]{1,0:T(8,128)(2,1)S(1)}, bf16[8,8192]{1,0:T(8,128)(2,1)}, u32[]{:S(2)}) copy-start(bf16[8,8192]{1,0:T(8,128)(2,1)} %v_hbm.1) | copy-start | bytes 393220
  2.7 0.8 %copy-start.3 = (bf16[2,128,128]{2,1,0:T(8,128)(2,1)S(1)}, bf16[2,128,128]{2,1,0:T(8,128)(2,1)}, u32[]{:S(2)}) copy-start(bf16[2,128,128]{2,1,0:T(8,128)(2,1)} %ctx_hbm.1) | copy-start | bytes 196612
  3.6 0.8 %copy-start.4 = (f32[64,128]{1,0:T(8,128)S(1)}, f32[64,128]{1,0:T(8,128)}, u32[]{:S(2)}) copy-start(f32[64,128]{1,0:T(8,128)} %gate_hbm.1) | copy-start | bytes 98308
  4.3 0.8 %copy-start.5 = (s32[8,1024]{1,0:T(8,128)S(1)}, s32[8,1024]{1,0:T(8,128)}, u32[]{:S(2)}) copy-start(s32[8,1024]{1,0:T(8,128)} %mask_hbm.1) | copy-start | bytes 98308
  5.1 0.7 %copy-start.6 = (s32[8]{0:T(128)S(1)}, s32[8]{0:T(128)}, u32[]{:S(2)}) copy-start(s32[8]{0:T(128)} %order_hbm.1) | copy-start | bytes 100
  5.7 0.7 %copy-start.7 = (s32[8]{0:T(128)S(1)}, s32[8]{0:T(128)}, u32[]{:S(2)}) copy-start(s32[8]{0:T(128)} %step_hbm.1) | copy-start | bytes 100

commit v2 on v1

v2 whole, which is shorter than its diff:
```python
import jax
import jax.numpy as jnp
from jax import lax
from jax.experimental import pallas as pl
from jax.experimental.pallas import tpu as pltpu
from jax.sharding import PartitionSpec as P

MESH = pl.DeviceIdType.MESH
NEG_FILL = -1e30
LOG2E = 1.4426950408889634
HD = 128
Y_OFFSETS = (2, 1, 3, 0)
K_EARLY = (3, 1, 2, 0)
K_LATE = (3, 2, 1, 0)


def kernel(q_hbm, k_hbm, v_hbm, ctx_hbm, gate_hbm, order_hbm, step_hbm, mask_hbm, out_ref,
           q_in, k_in, v_in, ctx_in, gate_in, order_s, step_s, mask_in,
           kv_out, ctx_out, kv, q_rows, gate_sib, out_rows, ctx_bias,
           load_sem, own_sem, left_sem, right_sem, far_sem, sib_sem, misc_sem, send_sem,
           open_sem):
    span, seq = lax.axis_index("span"), lax.axis_index("seq")
    x, yl = span // 2, span % 2
    yh, z, k = seq // 16, (seq // 2) % 8, seq % 2
    y = yh * 2 + yl
    stays = yl == k
    own = x * 2 + k
    early = z < 4
    left_x, right_x, far_x = (x + 3) % 4, (x + 1) % 4, (x + 2) % 4

    def device(x_, y_, z_, k_):
        return (x_ * 2 + y_ % 2, (y_ // 2) * 16 + z_ * 2 + k_)

    left, right = device(left_x, y, z, k), device(right_x, y, z, k)
    sibling = device(x, y, z, 1 - k)

    def remote(src, dst, sent, got, to):
        return pltpu.make_async_remote_copy(
            src_ref=src, dst_ref=dst, send_sem=sent, recv_sem=got, device_id=to, device_id_type=MESH
        )

    def wait_for(ref, sem):
        pltpu.make_async_copy(ref, ref, sem).wait()

    def signal(sem, to):
        pl.semaphore_signal(sem, inc=1, device_id=to, device_id_type=MESH)

    barrier = pltpu.get_barrier_semaphore()
    hears = jnp.where(early, 0, 1)
    for b in (4, 5, 3, 7, 6, 2, 1, 0):
        for a in Y_OFFSETS:
            to = (x * 2 + k, (seq - k + hears) ^ (a * 16 + b * 2))
            if a or b:
                signal(barrier, to)
            else:
                @pl.when(jnp.logical_not(stays & (k == hears)))
                def _():
                    signal(barrier, to)

    for x_ in (left_x, right_x):
        signal(barrier, device(x_, y, z, 0))

    @pl.when(k == 1)
    def _():
        signal(barrier, sibling)

    loads = [
        pltpu.make_async_copy(src, dst, load_sem.at[i])
        for i, (src, dst) in enumerate(
            [(k_hbm, k_in), (v_hbm, v_in), (ctx_hbm, ctx_in), (q_hbm, q_in), (gate_hbm, gate_in),
             (order_hbm, order_s), (step_hbm, step_s), (mask_hbm, mask_in)]
        )
    ]
    for load in loads:
        load.start()

    for load in loads[:3]:
        load.wait()
    for h in range(64):
        kv_out[h, 0] = k_in[:, h * HD:(h + 1) * HD]
        kv_out[h, 1] = v_in[:, h * HD:(h + 1) * HD]
    ctx_out[...] = ctx_in[...].reshape(ctx_out.shape)
    for load in loads[3:]:
        load.wait()

    @pl.when(k == 0)
    def _():
        pl.semaphore_wait(barrier, 37 - (early & (yl == 0)).astype(jnp.int32))
        signal(open_sem, sibling)

    @pl.when(k == 1)
    def _():
        pl.semaphore_wait(open_sem, 1)

    def await_late_rows():
        @pl.when(k == 1)
        def _():
            pl.semaphore_wait(barrier, 32 - (jnp.logical_not(early) & (yl == 1)).astype(jnp.int32))
            signal(open_sem, sibling)

        @pl.when(k == 0)
        def _():
            pl.semaphore_wait(open_sem, 1)

    gate_copy = remote(gate_in, gate_sib, misc_sem.at[0], misc_sem.at[1], sibling)
    gate_copy.start()

    def send_context():
        @pl.when(stays)
        def _():
            pltpu.make_async_copy(ctx_out, kv.at[:, own, 0], own_sem.at[0]).start()

        @pl.when(jnp.logical_not(stays))
        def _():
            remote(ctx_out, kv.at[:, span, 0], send_sem.at[0], own_sem.at[0], device(x, yh * 2 + k, z, yl)).start()

    head = (seq - k) + yl

    def send(src_of, dst, sent, got, b, may_stay):
        for a in Y_OFFSETS:
            for al in (1, 0):
                to = head ^ (a * 16 + b * 2 + al)
                src = src_of(to)
                device_id = (span ^ al, head ^ (a * 16 + b * 2))
                if a or al or not may_stay:
                    remote(src, dst(a), sent, got, device_id).start()
                else:
                    here = stays & (b == 0)

                    @pl.when(here)
                    def _():
                        pltpu.make_async_copy(src, dst(a), got).start()

                    @pl.when(jnp.logical_not(here))
                    def _():
                        remote(src, dst(a), sent, got, device_id).start()

    def send_keys(b, may_stay):
        group = b // 2
        send(lambda h: kv_out.at[h], lambda a: kv.at[:, span, 1 + group, b % 2 * 8 + 2 * a + k],
             send_sem.at[1], own_sem.at[1 + group], b, may_stay)

    def send_queries(b, may_stay):
        send(lambda h: q_in.at[:, pl.ds(pl.multiple_of(h * HD, HD), HD)], lambda a: q_rows.at[b * 8 + 2 * a + k],
             send_sem.at[2], misc_sem.at[2], b, may_stay)

    to_early = jnp.where(early, 0, 4)
    to_late = 4 - to_early

    def to_sibling(ref, kind, slot):
        remote(ref, ref, send_sem.at[4], sib_sem.at[kind, slot // 4], sibling).start()

    def pass_own(slot):
        ref = kv.at[:, own, slot]
        wait_for(ref, own_sem.at[slot])
        remote(ref, ref, send_sem.at[3], left_sem.at[slot], right).start()
        remote(ref, ref, send_sem.at[3], right_sem.at[slot], left).start()
        to_sibling(ref, 0, slot)

    def pass_near(slot):
        from_left, from_right = kv.at[:, left_x * 2 + k, slot], kv.at[:, right_x * 2 + k, slot]
        wait_for(from_left, left_sem.at[slot])
        half = kv.at[0, left_x * 2 + k, slot]
        remote(half, half, send_sem.at[3], far_sem.at[slot, 0], right).start()
        to_sibling(from_left, 1, slot)
        wait_for(from_right, right_sem.at[slot])
        half = kv.at[1, right_x * 2 + k, slot]
        remote(half, half, send_sem.at[3], far_sem.at[slot, 1], left).start()
        to_sibling(from_right, 2, slot)

    def pass_far(slot):
        ref = kv.at[:, far_x * 2 + k, slot]
        wait_for(kv.at[0, far_x * 2 + k, slot], far_sem.at[slot, 0])
        wait_for(kv.at[1, far_x * 2 + k, slot], far_sem.at[slot, 1])
        to_sibling(ref, 3, slot)

    scale = (HD ** -0.5) * LOG2E
    own_order = order_s[own]
    is_own = lax.broadcasted_iota(jnp.int32, (8, HD), 0) == own
    for s in range(8):
        seen = jnp.sum(jnp.where(is_own, mask_in[:, s * HD:(s + 1) * HD], 0), 0, keepdims=True)
        ctx_bias[s:s + 1, :] = jnp.where(seen == 1, 0.0, NEG_FILL)

    def span_bias(s, n):
        visible = (order_s[s] < own_order) | (s == own)
        return jnp.full((1, n), jnp.where(visible, 0.0, NEG_FILL), jnp.float32)

    def attend(state, spans, groups, bias):
        keys = kv[0, spans, groups].reshape(1024, HD)
        values = kv[1, spans, groups].reshape(1024, HD)
        scores = lax.dot_general(queries, keys, (((1,), (1,)), ((), ())), preferred_element_type=jnp.float32)
        scores = scores * scale + bias
        peak = jnp.max(scores, 1, keepdims=True)
        if state is not None:
            peak = jnp.maximum(state[0], peak)
        weights = jnp.exp2(scores - peak)
        total = weights[:, 0:HD]
        for t in range(1, 8):
            total = total + weights[:, t * HD:(t + 1) * HD]
        mixed = jnp.dot(weights.astype(jnp.bfloat16), values, preferred_element_type=jnp.float32)
        if state is not None:
            rescale = jnp.exp2(state[0] - peak)
            total = total + state[1] * rescale
            mixed = mixed + state[2] * rescale
        return peak, total, mixed

    def attend_early(state, x_):
        parts = []
        for c in range(2):
            parts += [ctx_bias[pl.ds(x_ * 2 + c, 1), :], span_bias(x_ * 2 + c, 384)]
        return attend(state, pl.ds(x_ * 2, 2), slice(0, 4), jnp.concatenate(parts, axis=1))

    def attend_last(state):
        return attend(state, slice(0, 8), 4, jnp.concatenate([span_bias(s, 128) for s in range(8)], axis=1))

    def sibling_early(kind):
        wait_for(kv.at[:, 0, pl.ds(0, 4)], sib_sem.at[kind, 0])

    @pl.when(early)
    def _():
        send_context()

    for i in K_EARLY:
        send_keys(to_early + i, i == 0)
    await_late_rows()

    @pl.when(jnp.logical_not(early))
    def _():
        send_context()

    for i in K_LATE:
        send_keys(to_late + i, i == 0)
    for i in K_EARLY:
        send_queries(to_early + i, i == 0)
    for i in K_LATE:
        send_queries(to_late + i, i == 0)
    pass_own(0)
    pass_own(1)
    pass_own(2)
    pass_own(3)
    pass_own(4)
    pass_near(0)
    wait_for(q_rows, misc_sem.at[2])
    queries = q_rows[...].reshape(512, HD)
    sibling_early(0)
    state = attend_early(None, x)
    pass_near(1)
    pass_near(2)
    pass_near(3)
    sibling_early(1)
    state = attend_early(state, left_x)
    pass_near(4)
    pass_far(0)
    pass_far(1)
    sibling_early(2)
    state = attend_early(state, right_x)
    pass_far(2)
    pass_far(3)
    pass_far(4)
    sibling_early(3)
    state = attend_early(state, far_x)
    for kind in range(4):
        wait_for(kv.at[:, 0, 4], sib_sem.at[kind, 1])
    _, total, mixed = attend_last(state)

    gate_copy.wait()
    step = step_s[own]
    gate = jnp.where(stays, gate_in[pl.ds(step, 1), :], gate_sib[pl.ds(step, 1), :])
    mixture = mixed / jnp.sum(total, 1, keepdims=True)
    out_rows[...] = (mixture * gate).astype(jnp.bfloat16).reshape(out_rows.shape)

    dst = out_ref.at[:, pl.ds(pl.multiple_of(head * HD, HD), HD)]
    for b in (4, 5, 3, 7, 6, 2, 1, 0):
        for a in Y_OFFSETS:
            for k_ in range(2):
                src = out_rows.at[b * 8 + 2 * a + k_]
                to = (x * 2 + k, (seq - k + k_) ^ (a * 16 + b * 2))
                if a or b:
                    remote(src, dst, send_sem.at[5], misc_sem.at[3], to).start()
                else:
                    here = stays & (k == k_)

                    @pl.when(here)
                    def _():
                        pltpu.make_async_copy(src, dst, misc_sem.at[3]).start()

                    @pl.when(jnp.logical_not(here))
                    def _():
                        remote(src, dst, send_sem.at[5], misc_sem.at[3], to).start()

    wait_for(kv.at[:, pl.ds(0, 3)], send_sem.at[3])
    wait_for(kv.at[:, pl.ds(0, 4)], send_sem.at[4])

    @pl.when(stays)
    def _():
        wait_for(kv_out.at[pl.ds(0, 63)], send_sem.at[1])
        wait_for(q_rows.at[pl.ds(0, 63)], send_sem.at[2])
        wait_for(out_rows.at[pl.ds(0, 63)], send_sem.at[5])

    @pl.when(jnp.logical_not(stays))
    def _():
        wait_for(ctx_out, send_sem.at[0])
        wait_for(kv_out, send_sem.at[1])
        wait_for(q_rows, send_sem.at[2])
        wait_for(out_rows, send_sem.at[5])

    wait_for(out_rows, misc_sem.at[3])


def local(*args):
    bf16 = jnp.bfloat16
    in_hbm = pl.BlockSpec(memory_space=pltpu.HBM)
    dma = pltpu.SemaphoreType.DMA
    return pl.pallas_call(
        kernel,
        out_shape=jax.ShapeDtypeStruct((8, 8192), bf16),
        in_specs=[in_hbm] * 8,
        out_specs=pl.BlockSpec(memory_space=pltpu.VMEM),
        scratch_shapes=[
            pltpu.VMEM((8, 8192), bf16),
            pltpu.VMEM((8, 8192), bf16),
            pltpu.VMEM((8, 8192), bf16),
            pltpu.VMEM((2, 128, HD), bf16),
            pltpu.VMEM((64, HD), jnp.float32),
            pltpu.SMEM((8,), jnp.int32),
            pltpu.SMEM((8,), jnp.int32),
            pltpu.VMEM((8, 1024), jnp.int32),
            pltpu.VMEM((64, 2, 8, HD), bf16),
            pltpu.VMEM((2, 16, 8, HD), bf16),
            pltpu.VMEM((2, 8, 5, 16, 8, HD), bf16),
            pltpu.VMEM((64, 8, HD), bf16),
            pltpu.VMEM((64, HD), jnp.float32),
            pltpu.VMEM((64, 8, HD), bf16),
            pltpu.VMEM((8, 128), jnp.float32),
            dma((8,)),
            dma((5,)),
            dma((5,)),
            dma((5,)),
            dma((5, 2)),
            dma((4, 2)),
            dma((4,)),
            dma((6,)),
            pltpu.SemaphoreType.REGULAR,
        ],
        compiler_params=pltpu.CompilerParams(
            collective_id=0, has_side_effects=True, vmem_limit_bytes=60 << 20
        ),
        cost_estimate=pl.CostEstimate(flops=1342177280, bytes_accessed=1 << 20, transcendentals=2621440),
        name="span_attention",
    )(*args)


def solution(mesh):
    rows = P(("span", "seq"), None)
    placed = (rows, rows, rows, P(None, "span", "seq"), P(None, "seq"), P(), P(), P())
    return jax.shard_map(local, mesh=mesh, in_specs=placed, out_specs=rows, check_vma=False)
```

time: 59 us -> 51.1 us (0.87)
  local copies, waits for them, and re-layouts: 7.03 us -> 1.57 us
  Pallas kernels: 51.5 us -> 49.4 us
    unnamed x17 -> x1, local copies, waits for them, and re-layouts: 7.03 us -> 1.57 us
    pallas_call x1, Pallas kernels: 51.5 us -> 49.4 us  [local(): pl.pallas_call(kernel, out_shape=jax.ShapeDtypeStruct((8, 8192), bf16), i...]
where the time goes in v2:
time: 51.1 us; the launch traced here: 51 us
  Pallas kernels  49.4 us (97%)
  local copies, waits for them, and re-layouts  1.57 us (3%)
    pallas_call x1, Pallas kernels, local(): pl.pallas_call(kernel, out_shape=jax.ShapeDtypeStruct((8, 8192), bf16), i...  49.4 us
    unnamed x1, local copies, waits for them, and re-layouts  1.57 us

profile of v2, /device:TPU:1, one launch (start us, length us, event | category | flops | bytes accessed | tf_op | source)
XLA Modules:
  0.0 51.0 jit_solution(9004120213901822298)
XLA Ops:
  0.0 49.4 %span_attention.1 = bf16[8,8192]{1,0:T(8,128)(2,1)} custom-call(bf16[8,8192]{1,0:T(8,128)(2,1)} %q_hbm.1, bf16[8,8192]{1,0:T(8,128)(2,1)} %k_hbm.1, bf16[8,8192]{1,0:T(8,128)(2,1)} %v_hbm.1, bf16[2,128,128]{2,1,0:T(8,128)(2,1)} %ctx_hbm.1, f32[64,128]{1,0:T(8,128)} %gate_hbm.1, s32[8]{0:T(128)} %order_hbm.1, s32[8]{0:T(128)} %step_hbm.1, s32[8,1024]{1,0:T(8,128)} %mask_hbm.1), custom_call_target="tpu_custom_call" | custom-call | flops 1342177280 | bytes 1048576 | tf_op jit(solution)/shard_map/span_attention/pallas_call | solution.py:314
  49.4 1.6 %copy.10 = bf16[8,8192]{1,0:T(8,128)(2,1)} copy(bf16[8,8192]{1,0:T(8,128)(2,1)} %span_attention.1) | data formatting | bytes 262144

commit v3 on v2

v3 whole, which is shorter than its diff:
```python
import jax
import jax.numpy as jnp
from jax import lax
from jax.experimental import pallas as pl
from jax.experimental.pallas import tpu as pltpu
from jax.sharding import PartitionSpec as P

MESH = pl.DeviceIdType.MESH
NEG_FILL = -1e30
LOG2E = 1.4426950408889634
HD = 128
Y_OFFSETS = (2, 1, 3, 0)
FIRST = 2


def kernel(q_hbm, k_hbm, v_hbm, ctx_hbm, gate_hbm, order_hbm, step_hbm, mask_hbm, out_ref,
           q_in, k_in, v_in, ctx_in, gate_in, order_s, step_s, mask_in,
           qkv_out, ctx_out, mine, kv, gate_sib, out_rows, ctx_bias,
           load_sem, own_sem, left_sem, right_sem, far_sem, sib_sem, here_sem, misc_sem, send_sem,
           open_sem):
    span, seq = lax.axis_index("span"), lax.axis_index("seq")
    x, yl = span // 2, span % 2
    yh, z, k = seq // 16, (seq // 2) % 8, seq % 2
    y = yh * 2 + yl
    stays = yl == k
    own = x * 2 + k
    early = z < 4
    left_x, right_x, far_x = (x + 3) % 4, (x + 1) % 4, (x + 2) % 4

    def device(x_, y_, z_, k_):
        return (x_ * 2 + y_ % 2, (y_ // 2) * 16 + z_ * 2 + k_)

    left, right = device(left_x, y, z, k), device(right_x, y, z, k)
    sibling = device(x, y, z, 1 - k)

    def remote(src, dst, sent, got, to):
        return pltpu.make_async_remote_copy(
            src_ref=src, dst_ref=dst, send_sem=sent, recv_sem=got, device_id=to, device_id_type=MESH
        )

    def wait_for(ref, sem):
        pltpu.make_async_copy(ref, ref, sem).wait()

    def signal(sem, to):
        pl.semaphore_signal(sem, inc=1, device_id=to, device_id_type=MESH)

    barrier = pltpu.get_barrier_semaphore()
    hears = jnp.where(early, 0, 1)
    for b in (4, 5, 3, 7, 6, 2, 1, 0):
        for a in Y_OFFSETS:
            to = (x * 2 + k, (seq - k + hears) ^ (a * 16 + b * 2))
            if a or b:
                signal(barrier, to)
            else:
                @pl.when(jnp.logical_not(stays & (k == hears)))
                def _():
                    signal(barrier, to)

    for x_ in (left_x, right_x):
        signal(barrier, device(x_, y, z, 0))

    @pl.when(k == 1)
    def _():
        signal(barrier, sibling)

    loads = [
        pltpu.make_async_copy(src, dst, load_sem.at[i])
        for i, (src, dst) in enumerate(
            [(k_hbm, k_in), (v_hbm, v_in), (q_hbm, q_in), (ctx_hbm, ctx_in), (gate_hbm, gate_in),
             (order_hbm, order_s), (step_hbm, step_s), (mask_hbm, mask_in)]
        )
    ]
    for load in loads:
        load.start()

    for load in loads[:4]:
        load.wait()
    for h in range(64):
        for t, ref in enumerate((k_in, v_in, q_in)):
            qkv_out[h, t] = ref[:, h * HD:(h + 1) * HD]
    for t in range(2):
        ctx_out[:, t] = ctx_in[t].reshape(16, 8, HD)
    for load in loads[4:]:
        load.wait()

    @pl.when(k == 0)
    def _():
        pl.semaphore_wait(barrier, 37 - (early & (yl == 0)).astype(jnp.int32))
        signal(open_sem, sibling)

    @pl.when(k == 1)
    def _():
        pl.semaphore_wait(open_sem, 1)

    def await_late_rows():
        @pl.when(k == 1)
        def _():
            pl.semaphore_wait(barrier, 32 - (jnp.logical_not(early) & (yl == 1)).astype(jnp.int32))
            signal(open_sem, sibling)

        @pl.when(k == 0)
        def _():
            pl.semaphore_wait(open_sem, 1)

    gate_copy = remote(gate_in, gate_sib, misc_sem.at[0], misc_sem.at[1], sibling)
    gate_copy.start()

    def send_context():
        @pl.when(stays)
        def _():
            pltpu.make_async_copy(ctx_out, kv.at[own, 0], own_sem.at[0]).start()

        @pl.when(jnp.logical_not(stays))
        def _():
            remote(ctx_out, kv.at[span, 0], send_sem.at[0], own_sem.at[0], device(x, yh * 2 + k, z, yl)).start()

    head = (seq - k) + yl

    def send(b, may_stay):
        got = own_sem.at[1 + b // 2]
        for a in Y_OFFSETS:
            dst = mine.at[b // 2, b % 2 * 8 + 2 * a + k]
            for al in (1, 0):
                src = qkv_out.at[head ^ (a * 16 + b * 2 + al)]
                device_id = (span ^ al, head ^ (a * 16 + b * 2))
                if a or al or not may_stay:
                    remote(src, dst, send_sem.at[1], got, device_id).start()
                else:
                    here = stays & (b == 0)

                    @pl.when(here)
                    def _():
                        pltpu.make_async_copy(src, dst, got).start()

                    @pl.when(jnp.logical_not(here))
                    def _():
                        remote(src, dst, send_sem.at[1], got, device_id).start()

    to_early = jnp.where(early, 0, 4)
    to_late = 4 - to_early

    def to_sibling(src, s, slot, kind):
        remote(src, kv.at[s, slot], send_sem.at[4], sib_sem.at[kind, int(slot >= FIRST)], sibling).start()

    def pass_own(slot):
        dst = kv.at[own, slot]
        if slot:
            wait_for(mine.at[slot - 1], own_sem.at[slot])
            src = mine.at[slot - 1, :, pl.ds(0, 2)]
            pltpu.make_async_copy(src, dst, here_sem.at[int(slot >= FIRST)]).start()
        else:
            wait_for(dst, own_sem.at[slot])
            src = dst
        remote(src, dst, send_sem.at[3], left_sem.at[slot], right).start()
        remote(src, dst, send_sem.at[3], right_sem.at[slot], left).start()
        to_sibling(src, own, slot, 0)

    def pass_near(slot):
        for t, (x_, got, to) in enumerate(((left_x, left_sem, right), (right_x, right_sem, left))):
            s = x_ * 2 + k
            wait_for(kv.at[s, slot], got.at[slot])
            half = kv.at[s, slot, :, t]
            remote(half, half, send_sem.at[3], far_sem.at[slot, t], to).start()
            to_sibling(kv.at[s, slot], s, slot, 1 + t)

    def pass_far(slot):
        s = far_x * 2 + k
        for t in range(2):
            wait_for(kv.at[s, slot, :, t], far_sem.at[slot, t])
        to_sibling(kv.at[s, slot], s, slot, 3)

    scale = (HD ** -0.5) * LOG2E
    own_order = order_s[own]
    is_own = lax.broadcasted_iota(jnp.int32, (8, HD), 0) == own
    for s in range(8):
        seen = jnp.sum(jnp.where(is_own, mask_in[:, s * HD:(s + 1) * HD], 0), 0, keepdims=True)
        ctx_bias[s:s + 1, :] = jnp.where(seen == 1, 0.0, NEG_FILL)

    def span_bias(s, n):
        visible = (order_s[s] < own_order) | (s == own)
        return jnp.full((1, n), jnp.where(visible, 0.0, NEG_FILL), jnp.float32)

    def attend(state, x_, groups, bias):
        spans = pl.ds(x_ * 2, 2)
        keys = kv[spans, groups, :, 0].reshape(bias.shape[1], HD)
        values = kv[spans, groups, :, 1].reshape(bias.shape[1], HD)
        scores = lax.dot_general(queries, keys, (((1,), (1,)), ((), ())), preferred_element_type=jnp.float32)
        scores = scores * scale + bias
        peak = jnp.max(scores, 1, keepdims=True)
        if state is not None:
            peak = jnp.maximum(state[0], peak)
        weights = jnp.exp2(scores - peak)
        total = weights[:, 0:HD]
        for t in range(1, bias.shape[1] // HD):
            total = total + weights[:, t * HD:(t + 1) * HD]
        mixed = jnp.dot(weights.astype(jnp.bfloat16), values, preferred_element_type=jnp.float32)
        if state is not None:
            rescale = jnp.exp2(state[0] - peak)
            total = total + state[1] * rescale
            mixed = mixed + state[2] * rescale
        return peak, total, mixed

    def attend_first(state, kind, x_):
        wait_for(kv.at[0, pl.ds(0, FIRST)], sib_sem.at[kind, 0])
        parts = []
        for c in range(2):
            parts += [ctx_bias[pl.ds(x_ * 2 + c, 1), :], span_bias(x_ * 2 + c, (FIRST - 1) * 128)]
        return attend(state, x_, slice(0, FIRST), jnp.concatenate(parts, axis=1))

    def attend_rest(state, kind, x_):
        wait_for(kv.at[0, pl.ds(FIRST, 5 - FIRST)], sib_sem.at[kind, 1])
        parts = [span_bias(x_ * 2 + c, (5 - FIRST) * 128) for c in range(2)]
        return attend(state, x_, slice(FIRST, 5), jnp.concatenate(parts, axis=1))

    @pl.when(early)
    def _():
        send_context()


    @pl.when(early)
    def _():
        for i in (3, 2, 1, 0):
            send(to_early + i, i == 0)


    @pl.when(jnp.logical_not(early))
    def _():
        for i in (0,):
            send(to_early + i, False)

    await_late_rows()

    @pl.when(jnp.logical_not(early))
    def _():
        send_context()

    for i in (0, 1, 2, 3):
        send(to_late + i, i == 0)

    @pl.when(jnp.logical_not(early))
    def _():
        for i in (1, 3, 2):
            send(to_early + i, False)

    pass_own(0)
    pass_own(1)
    pass_near(0)
    pass_own(2)
    pass_own(3)
    pass_own(4)
    pass_near(1)
    queries = mine[:, :, 2].reshape(512, HD)
    wait_for(kv.at[0, pl.ds(0, FIRST - 1)], here_sem.at[0])
    wait_for(kv.at[0, pl.ds(0, 5 - FIRST)], here_sem.at[1])
    state = attend_first(None, 0, x)
    state = attend_first(state, 1, left_x)
    pass_near(2)
    pass_near(3)
    pass_near(4)
    state = attend_rest(state, 0, x)
    pass_far(0)
    pass_far(1)
    pass_far(2)
    state = attend_first(state, 2, right_x)
    state = attend_first(state, 3, far_x)
    pass_far(3)
    pass_far(4)
    state = attend_rest(state, 1, left_x)
    state = attend_rest(state, 2, right_x)
    state = attend_rest(state, 3, far_x)
    _, total, mixed = state

    gate_copy.wait()
    step = step_s[own]
    gate = jnp.where(stays, gate_in[pl.ds(step, 1), :], gate_sib[pl.ds(step, 1), :])
    mixture = mixed / jnp.sum(total, 1, keepdims=True)
    out_rows[...] = (mixture * gate).astype(jnp.bfloat16).reshape(out_rows.shape)

    dst = out_ref.at[:, pl.ds(pl.multiple_of(head * HD, HD), HD)]
    for b in (4, 5, 3, 7, 6, 2, 1, 0):
        for a in Y_OFFSETS:
            for k_ in range(2):
                src = out_rows.at[b * 8 + 2 * a + k_]
                to = (x * 2 + k, (seq - k + k_) ^ (a * 16 + b * 2))
                if a or b:
                    remote(src, dst, send_sem.at[5], misc_sem.at[3], to).start()
                else:
                    here = stays & (k == k_)

                    @pl.when(here)
                    def _():
                        pltpu.make_async_copy(src, dst, misc_sem.at[3]).start()

                    @pl.when(jnp.logical_not(here))
                    def _():
                        remote(src, dst, send_sem.at[5], misc_sem.at[3], to).start()

    wait_for(kv.at[pl.ds(0, 3)], send_sem.at[3])
    wait_for(kv.at[pl.ds(0, 4)], send_sem.at[4])

    @pl.when(stays)
    def _():
        wait_for(qkv_out.at[pl.ds(0, 63)], send_sem.at[1])
        wait_for(out_rows.at[pl.ds(0, 63)], send_sem.at[5])

    @pl.when(jnp.logical_not(stays))
    def _():
        wait_for(ctx_out, send_sem.at[0])
        wait_for(qkv_out, send_sem.at[1])
        wait_for(out_rows, send_sem.at[5])

    wait_for(out_rows, misc_sem.at[3])


def local(*args):
    bf16 = jnp.bfloat16
    in_hbm = pl.BlockSpec(memory_space=pltpu.HBM)
    dma = pltpu.SemaphoreType.DMA
    return pl.pallas_call(
        kernel,
        out_shape=jax.ShapeDtypeStruct((8, 8192), bf16),
        in_specs=[in_hbm] * 8,
        out_specs=pl.BlockSpec(memory_space=pltpu.HBM),
        scratch_shapes=[
            pltpu.VMEM((8, 8192), bf16),
            pltpu.VMEM((8, 8192), bf16),
            pltpu.VMEM((8, 8192), bf16),
            pltpu.VMEM((2, 128, HD), bf16),
            pltpu.VMEM((64, HD), jnp.float32),
            pltpu.SMEM((8,), jnp.int32),
            pltpu.SMEM((8,), jnp.int32),
            pltpu.VMEM((8, 1024), jnp.int32),
            pltpu.VMEM((64, 3, 8, HD), bf16),
            pltpu.VMEM((16, 2, 8, HD), bf16),
            pltpu.VMEM((4, 16, 3, 8, HD), bf16),
            pltpu.VMEM((8, 5, 16, 2, 8, HD), bf16),
            pltpu.VMEM((64, HD), jnp.float32),
            pltpu.VMEM((64, 8, HD), bf16),
            pltpu.VMEM((8, 128), jnp.float32),
            dma((8,)),
            dma((5,)),
            dma((5,)),
            dma((5,)),
            dma((5, 2)),
            dma((4, 2)),
            dma((2,)),
            dma((4,)),
            dma((6,)),
            pltpu.SemaphoreType.REGULAR,
        ],
        compiler_params=pltpu.CompilerParams(
            collective_id=0, has_side_effects=True, vmem_limit_bytes=60 << 20
        ),
        cost_estimate=pl.CostEstimate(flops=1342177280, bytes_accessed=1 << 20, transcendentals=2621440),
        name="span_attention",
    )(*args)


def solution(mesh):
    rows = P(("span", "seq"), None)
    placed = (rows, rows, rows, P(None, "span", "seq"), P(None, "seq"), P(), P(), P())
    return jax.shard_map(local, mesh=mesh, in_specs=placed, out_specs=rows, check_vma=False)
```

time: 51.1 us -> 50.1 us (0.980)
  Pallas kernels: 49.4 us -> 48.4 us
    pallas_call x1, Pallas kernels: 49.4 us -> 48.4 us  [local(): pl.pallas_call(kernel, out_shape=jax.ShapeDtypeStruct((8, 8192), bf16), i...]
where the time goes in v3:
time: 50.1 us; the launch traced here: 50 us
  Pallas kernels  48.4 us (97%)
  local copies, waits for them, and re-layouts  1.57 us (3%)
    pallas_call x1, Pallas kernels, local(): pl.pallas_call(kernel, out_shape=jax.ShapeDtypeStruct((8, 8192), bf16), i...  48.4 us
    unnamed x1, local copies, waits for them, and re-layouts  1.57 us

profile of v3, /device:TPU:1, one launch (start us, length us, event | category | flops | bytes accessed | tf_op | source)
XLA Modules:
  0.0 50.0 jit_solution(173697860393041672)
XLA Ops:
  0.0 48.4 %span_attention.1 = bf16[8,8192]{1,0:T(8,128)(2,1)} custom-call(bf16[8,8192]{1,0:T(8,128)(2,1)} %q_hbm.1, bf16[8,8192]{1,0:T(8,128)(2,1)} %k_hbm.1, bf16[8,8192]{1,0:T(8,128)(2,1)} %v_hbm.1, bf16[2,128,128]{2,1,0:T(8,128)(2,1)} %ctx_hbm.1, f32[64,128]{1,0:T(8,128)} %gate_hbm.1, s32[8]{0:T(128)} %order_hbm.1, s32[8]{0:T(128)} %step_hbm.1, s32[8,1024]{1,0:T(8,128)} %mask_hbm.1), custom_call_target="tpu_custom_call" | custom-call | flops 1342177280 | bytes 1048576 | tf_op jit(solution)/shard_map/span_attention/pallas_call | solution.py:319
  48.4 1.6 %copy.10 = bf16[8,8192]{1,0:T(8,128)(2,1)} copy(bf16[8,8192]{1,0:T(8,128)(2,1)} %span_attention.1) | data formatting | bytes 262144

commit v4 on v3

--- a/solution.py
+++ b/solution.py
@@ -273,11 +273,12 @@
     gate_copy.wait()
     step = step_s[own]
     gate = jnp.where(stays, gate_in[pl.ds(step, 1), :], gate_sib[pl.ds(step, 1), :])
-    mixture = mixed / jnp.sum(total, 1, keepdims=True)
-    out_rows[...] = (mixture * gate).astype(jnp.bfloat16).reshape(out_rows.shape)
 
     dst = out_ref.at[:, pl.ds(pl.multiple_of(head * HD, HD), HD)]
     for b in (4, 5, 3, 7, 6, 2, 1, 0):
+        rows = slice(b * 64, (b + 1) * 64)
+        mixture = mixed[rows] / jnp.sum(total[rows], 1, keepdims=True)
+        out_rows[b * 8:(b + 1) * 8] = (mixture * gate).astype(jnp.bfloat16).reshape(8, 8, HD)
         for a in Y_OFFSETS:
             for k_ in range(2):
                 src = out_rows.at[b * 8 + 2 * a + k_]

time: 50.1 us -> 50.1 us (level)
  no operation moved by 1% of the time
where the time goes in v4:
time: 50.1 us; the launch traced here: 49.9 us
  Pallas kernels  48.3 us (96%)
  local copies, waits for them, and re-layouts  1.57 us (3%)
    pallas_call x1, Pallas kernels, local(): pl.pallas_call(kernel, out_shape=jax.ShapeDtypeStruct((8, 8192), bf16), i...  48.3 us
    unnamed x1, local copies, waits for them, and re-layouts  1.57 us

profile of v4, /device:TPU:1, one launch (start us, length us, event | category | flops | bytes accessed | tf_op | source)
XLA Modules:
  0.0 49.9 jit_solution(6326074204244179037)
XLA Ops:
  0.0 48.3 %span_attention.1 = bf16[8,8192]{1,0:T(8,128)(2,1)} custom-call(bf16[8,8192]{1,0:T(8,128)(2,1)} %q_hbm.1, bf16[8,8192]{1,0:T(8,128)(2,1)} %k_hbm.1, bf16[8,8192]{1,0:T(8,128)(2,1)} %v_hbm.1, bf16[2,128,128]{2,1,0:T(8,128)(2,1)} %ctx_hbm.1, f32[64,128]{1,0:T(8,128)} %gate_hbm.1, s32[8]{0:T(128)} %order_hbm.1, s32[8]{0:T(128)} %step_hbm.1, s32[8,1024]{1,0:T(8,128)} %mask_hbm.1), custom_call_target="tpu_custom_call" | custom-call | flops 1342177280 | bytes 1048576 | tf_op jit(solution)/shard_map/span_attention/pallas_call | solution.py:320
  48.4 1.6 %copy.10 = bf16[8,8192]{1,0:T(8,128)(2,1)} copy(bf16[8,8192]{1,0:T(8,128)(2,1)} %span_attention.1) | data formatting | bytes 262144
